TPU v7x, 128 devices: a whole 4x4x4 slice. The times are simulated.
128 devices in a mesh: blk: 16 (over z_hi, x, core), tp: 8 (over y, z_lo).
Axes of the slice: x: 4, y: 4, z: 4 (z_hi: 2, z_lo: 2; z = z_hi * 2 + z_lo), core: 2. Of those that a mesh axis runs over, the one named last changes fastest.
Arguments:
- act_rows: bfloat16 [8, 128, 524288], P('tp', None, 'blk'), may hold values from -6 to 6
- grad_rows: bfloat16 [8, 64, 524288], P('tp', None, 'blk'), may hold values from -0.59765625 to 0.59765625
- query_grads: bfloat16 [256, 8, 64, 128], P('blk', 'tp'), may hold values from -0.0234375 to 0.0234375
- ginv: float32 [8, 64, 64], P('tp'), as said below
- ainv: float32 [8, 128, 128], P('tp'), as said below
- lengths: int32 [128, 64], P(('blk', 'tp')), may hold values from 1 to 128, 4096 in all within a row
Outputs:
- scores: float32 [8192, 256], P(('blk', 'tp'))
Inputs may be any that keep to these rules, and one draw needn't show every extreme that they name: `lengths`: each row sums to 4096, and each row's largest entry is 128. `ginv`: Symmetric. `ainv`: Symmetric.
All inputs are finite; a program needn't handle non-finite values.
Results may differ from a plain program's by a relative error of at most 0.0041.
Values may be sent and summed in bfloat16 or wider, within the bound.
No kernel may reach another device: no remote copies, remote signals or barrier semaphores. Data moves between devices by JAX's collectives and lax.ppermute only.
A program may use at most 128 MiB of HBM per device.

v0:
```python
import jax
import jax.numpy as jnp
from jax import lax
from jax.sharding import PartitionSpec as P

MOST = 128


def passed_along(block, axis, distance):
    devices = range(lax.axis_size(axis))
    route = [((i - distance) % len(devices), i) for i in devices]
    return lax.ppermute(block, axis, route)


def doc_gradients(activations, gradients, doc_lengths):
    owner_rows = doc_lengths.shape[0]
    per_owner = activations.shape[2] // owner_rows
    bases = (jnp.arange(owner_rows, dtype=jnp.int32) * per_owner)[:, None]
    starts = (jnp.cumsum(doc_lengths, axis=1) - doc_lengths + bases).reshape(-1)
    flat_lengths = doc_lengths.reshape(-1)
    offsets_in = jnp.arange(MOST, dtype=jnp.int32)
    token_index = jnp.minimum(starts[:, None] + offsets_in[None, :], activations.shape[2] - 1)
    inside = (offsets_in[None, :] < flat_lengths[:, None]).astype(activations.dtype)
    picked_acts = jnp.take(activations, token_index, axis=2) * inside
    picked_grads = jnp.take(gradients, token_index, axis=2)
    outer_sums = jnp.einsum(
        "lgdm,ladm->dlga", picked_grads, picked_acts, preferred_element_type=jnp.float32
    )
    return outer_sums.astype(jnp.bfloat16).reshape(outer_sums.shape[0], -1)


def precondition(query_grads, ginv, ainv):
    left_side = jnp.einsum(
        "lgh,qlha->qlga", ginv, query_grads.astype(jnp.float32), precision=lax.Precision.HIGHEST
    )
    both_sides = jnp.einsum("qlga,lab->qlgb", left_side, ainv, precision=lax.Precision.HIGHEST)
    return both_sides.astype(jnp.bfloat16)


def circulate(documents, query_panel, rotate):
    cycle_size = lax.axis_size("blk")
    position = lax.axis_index("blk")
    panel_rows = query_panel.shape[0]
    initial = jnp.zeros((documents.shape[0], panel_rows * cycle_size), jnp.float32)

    def place_tile(score_block, current, rounds_done):
        score_tile = jnp.einsum("dk,qk->dq", documents, current, preferred_element_type=jnp.float32)
        column = (position - rounds_done) % cycle_size * panel_rows
        return lax.dynamic_update_slice(score_block, score_tile, (jnp.int32(0), column))

    def advance(rounds_done, carry):
        score_block, current = carry
        score_block = place_tile(score_block, current, rounds_done)
        return (score_block, rotate(current))

    score_block, current = lax.fori_loop(0, cycle_size - 1, advance, (initial, query_panel))
    return place_tile(score_block, current, cycle_size - 1)


def local(act_rows, grad_rows, query_grads, ginv, ainv, lengths):
    query_panel = precondition(query_grads, ginv, ainv)
    activations, gradients = (
        lax.all_to_all(act_rows, "tp", split_axis=2, concat_axis=0, tiled=True),
        lax.all_to_all(grad_rows, "tp", split_axis=2, concat_axis=0, tiled=True),
    )
    documents = doc_gradients(activations, gradients, lengths)
    full_panel = lax.all_gather(query_panel, "tp", axis=1, tiled=True)
    full_panel = full_panel.reshape(full_panel.shape[0], -1)

    def rotate(block):
        return passed_along(block, "blk", 1)

    return circulate(documents, full_panel, rotate)


def solution(mesh):
    placed = (
        P("tp", None, "blk"),
        P("tp", None, "blk"),
        P("blk", "tp", None, None),
        P("tp", None, None),
        P("tp", None, None),
        P(("blk", "tp"), None),
    )
    return jax.shard_map(
        local, mesh=mesh, in_specs=placed, out_specs=P(("blk", "tp"), None), check_vma=False
    )
```

profile of v0, /device:TPU:0, one launch (start us, length us, event | category | flops | bytes accessed | tf_op | source)
XLA Modules:
  0.0 1257.5 jit_solution(4657765128799890062)
XLA Ops:
  6.5 33.1 %copy.25 = bf16[1,64,32768]{1,0,2:T(2,128)(2,1)} copy(bf16[1,64,32768]{2,1,0:T(8,128)(2,1)} %param.9) | data formatting | bytes 8388608 | tf_op args[1]
  40.2 179.1 %reduce.1 = bf16[32768,64]{1,0:T(8,128)(2,1)} reduce(bf16[32768,1,64]{2,1,0:T(2,128)(2,1)} %bitcast.75, bf16[]{:T(256)} %broadcast.92), dimensions={1}, to_apply=%bitcast.57.reduce_sub_computation | reduce | bytes 8388610
  219.3 10.5 reshape.136
  236.0 34.0 %copy.29 = bf16[1,128,32768]{1,0,2:T(2,128)(2,1)} copy(bf16[1,128,32768]{2,1,0:T(8,128)(2,1)} %param.8) | data formatting | bytes 16777216 | tf_op args[0]
  270.0 179.0 %reduce = bf16[32768,128]{1,0:T(8,128)(2,1)} reduce(bf16[32768,1,128]{2,1,0:T(2,128)(2,1)} %bitcast.77, bf16[]{:T(256)} %broadcast.92), dimensions={1}, to_apply=%bitcast.55.reduce_sub_computation | reduce | bytes 16777218
  467.1 11.2 reshape.137
  486.4 25.1 %copy.57 = bf16[1,64,8,4096]{1,2,3,0:T(8,128)(2,1)} copy(bf16[1,64,8,4096]{1,3,2,0:T(8,128)(2,1)S(1)} %bitcast.81) | data formatting | bytes 8388608 | tf_op jit(solution)/shard_map/all_to_all | solution.py:64
  511.5 60.6 %gather_fusion = bf16[8192,8,64]{2,1,0:T(8,128)(2,1)} fusion(bf16[8,64,4096]{1,0,2:T(8,128)(2,1)} %bitcast.83, s32[8192]{0:T(1024)S(1)} %fusion.12), kind=kCustom, calls=%fused_computation | custom fusion | bytes 16809984 | tf_op jit(solution)/shard_map/jit(_take)/gather | solution.py:25
  572.2 16.7 %copy.38 = bf16[64,128,8,64]{1,0,3,2:T(8,128)(2,1)} copy(bf16[64,128,8,64]{3,2,1,0:T(8,128)(2,1)} %bitcast.80) | data formatting | bytes 16777216 | tf_op jit(solution)/shard_map/jit(_take)/gather | solution.py:25
  610.9 13.3 %reshape.135 = bf16[32768,1,128]{2,1,0:T(2,128)(2,1)} reshape(bf16[8,2,262144]{2,1,0:T(2,128)(2,1)} %all-to-all-done.1) | data formatting | bytes 16777216
  632.2 25.1 %copy.58 = bf16[1,128,8,4096]{1,2,3,0:T(8,128)(2,1)} copy(bf16[1,128,8,4096]{1,3,2,0:T(8,128)(2,1)S(1)} %bitcast.82) | data formatting | bytes 16777216 | tf_op jit(solution)/shard_map/all_to_all | solution.py:63
  657.4 60.5 %gather_fusion.1 = bf16[8192,8,128]{2,1,0:T(8,128)(2,1)} fusion(bf16[8,128,4096]{1,0,2:T(8,128)(2,1)} %bitcast.72, s32[8192]{0:T(1024)S(1)} %fusion.12), kind=kCustom, calls=%fused_computation.1 | custom fusion | bytes 33587200 | tf_op jit(solution)/shard_map/jit(_take)/gather | solution.py:24
  717.9 24.6 %multiply_bitcast_fusion = bf16[8,128,64,128]{1,0,3,2:T(8,128)(2,1)} fusion(bf16[64,128,8,128]{3,2,1,0:T(8,128)(2,1)} %bitcast.74, pred[64,128]{1,0:T(8,128)(4,1)S(1)} %get-tuple-element.151, bf16[64,128]{1,0:T(8,128)(2,1)S(1)} %get-tuple-element.152), kind=kLoop, calls=%fused_computation.5 | loop fusion | flops 16777216 | bytes 33579008 | tf_op jit(solution)/shard_map/mul | solution.py:24
  742.5 20.5 %fusion.3 = bf16[64,8,64,128]{3,2,1,0:T(8,128)(2,1)} fusion(bf16[8,128,64,128]{1,0,3,2:T(8,128)(2,1)} %multiply_bitcast_fusion, bf16[8,64,64,128]{3,2,1,0:T(8,128)(2,1)} %select_bitcast_fusion), kind=kOutput, calls=%fused_computation.11 | convolution fusion | flops 1077936128 | bytes 33554432 | tf_op jit(solution)/shard_map/lgdm,ladm->dlga/dot_general | solution.py:26
  763.1 12.0 copy.56
  775.1 461.8 %while.17 = (s32[]{:T(128)}, f32[64,256]{0,1:T(8,128)S(1)}, bf16[16,65536]{1,0:T(8,128)(2,1)}, bf16[64,65536]{1,0:T(8,128)(2,1)}, s32[]{:T(128)}, /*index=5*/s32...) while((s32[]{:T(128)}, f32[64,256]{0,1:T(8,128)S(1)}, bf16[16,65536]{1,0:T(8,128)(2,1)}, ...), condition=%wide.region_2.3_spmd, body=%wide.region_1.2_spmd.sunk | while | flops 134217744 | bytes 23077176 | solution.py:56
  782.3 23.5 %collective-permute-done = bf16[16,65536]{1,0:T(8,128)(2,1)} collective-permute-done((bf16[16,65536]{1,0:T(8,128)(2,1)S(1)}, bf16[16,65536]{1,0:T(8,128)(2,1)}, u32[]{:S(2)}, u32[]{:S(2)}) %collective-permute-start) | collective-permute-done | bytes 2097184 | tf_op jit(solution)/shard_map/while/body/eval_jaxpr/ppermute | solution.py:12
  813.1 23.5 %collective-permute-done = bf16[16,65536]{1,0:T(8,128)(2,1)} collective-permute-done((bf16[16,65536]{1,0:T(8,128)(2,1)S(1)}, bf16[16,65536]{1,0:T(8,128)(2,1)}, u32[]{:S(2)}, u32[]{:S(2)}) %collective-permute-start) | collective-permute-done | bytes 2097184 | tf_op jit(solution)/shard_map/while/body/eval_jaxpr/ppermute | solution.py:12
  843.9 23.5 %collective-permute-done = bf16[16,65536]{1,0:T(8,128)(2,1)} collective-permute-done((bf16[16,65536]{1,0:T(8,128)(2,1)S(1)}, bf16[16,65536]{1,0:T(8,128)(2,1)}, u32[]{:S(2)}, u32[]{:S(2)}) %collective-permute-start) | collective-permute-done | bytes 2097184 | tf_op jit(solution)/shard_map/while/body/eval_jaxpr/ppermute | solution.py:12
  874.6 23.5 %collective-permute-done = bf16[16,65536]{1,0:T(8,128)(2,1)} collective-permute-done((bf16[16,65536]{1,0:T(8,128)(2,1)S(1)}, bf16[16,65536]{1,0:T(8,128)(2,1)}, u32[]{:S(2)}, u32[]{:S(2)}) %collective-permute-start) | collective-permute-done | bytes 2097184 | tf_op jit(solution)/shard_map/while/body/eval_jaxpr/ppermute | solution.py:12
  905.4 23.5 %collective-permute-done = bf16[16,65536]{1,0:T(8,128)(2,1)} collective-permute-done((bf16[16,65536]{1,0:T(8,128)(2,1)S(1)}, bf16[16,65536]{1,0:T(8,128)(2,1)}, u32[]{:S(2)}, u32[]{:S(2)}) %collective-permute-start) | collective-permute-done | bytes 2097184 | tf_op jit(solution)/shard_map/while/body/eval_jaxpr/ppermute | solution.py:12
  936.2 23.5 %collective-permute-done = bf16[16,65536]{1,0:T(8,128)(2,1)} collective-permute-done((bf16[16,65536]{1,0:T(8,128)(2,1)S(1)}, bf16[16,65536]{1,0:T(8,128)(2,1)}, u32[]{:S(2)}, u32[]{:S(2)}) %collective-permute-start) | collective-permute-done | bytes 2097184 | tf_op jit(solution)/shard_map/while/body/eval_jaxpr/ppermute | solution.py:12
  967.0 23.5 %collective-permute-done = bf16[16,65536]{1,0:T(8,128)(2,1)} collective-permute-done((bf16[16,65536]{1,0:T(8,128)(2,1)S(1)}, bf16[16,65536]{1,0:T(8,128)(2,1)}, u32[]{:S(2)}, u32[]{:S(2)}) %collective-permute-start) | collective-permute-done | bytes 2097184 | tf_op jit(solution)/shard_map/while/body/eval_jaxpr/ppermute | solution.py:12
  997.7 23.5 %collective-permute-done = bf16[16,65536]{1,0:T(8,128)(2,1)} collective-permute-done((bf16[16,65536]{1,0:T(8,128)(2,1)S(1)}, bf16[16,65536]{1,0:T(8,128)(2,1)}, u32[]{:S(2)}, u32[]{:S(2)}) %collective-permute-start) | collective-permute-done | bytes 2097184 | tf_op jit(solution)/shard_map/while/body/eval_jaxpr/ppermute | solution.py:12
  1028.5 23.5 %collective-permute-done = bf16[16,65536]{1,0:T(8,128)(2,1)} collective-permute-done((bf16[16,65536]{1,0:T(8,128)(2,1)S(1)}, bf16[16,65536]{1,0:T(8,128)(2,1)}, u32[]{:S(2)}, u32[]{:S(2)}) %collective-permute-start) | collective-permute-done | bytes 2097184 | tf_op jit(solution)/shard_map/while/body/eval_jaxpr/ppermute | solution.py:12
  1059.3 23.5 %collective-permute-done = bf16[16,65536]{1,0:T(8,128)(2,1)} collective-permute-done((bf16[16,65536]{1,0:T(8,128)(2,1)S(1)}, bf16[16,65536]{1,0:T(8,128)(2,1)}, u32[]{:S(2)}, u32[]{:S(2)}) %collective-permute-start) | collective-permute-done | bytes 2097184 | tf_op jit(solution)/shard_map/while/body/eval_jaxpr/ppermute | solution.py:12
  1090.0 23.5 %collective-permute-done = bf16[16,65536]{1,0:T(8,128)(2,1)} collective-permute-done((bf16[16,65536]{1,0:T(8,128)(2,1)S(1)}, bf16[16,65536]{1,0:T(8,128)(2,1)}, u32[]{:S(2)}, u32[]{:S(2)}) %collective-permute-start) | collective-permute-done | bytes 2097184 | tf_op jit(solution)/shard_map/while/body/eval_jaxpr/ppermute | solution.py:12
  1120.8 23.5 %collective-permute-done = bf16[16,65536]{1,0:T(8,128)(2,1)} collective-permute-done((bf16[16,65536]{1,0:T(8,128)(2,1)S(1)}, bf16[16,65536]{1,0:T(8,128)(2,1)}, u32[]{:S(2)}, u32[]{:S(2)}) %collective-permute-start) | collective-permute-done | bytes 2097184 | tf_op jit(solution)/shard_map/while/body/eval_jaxpr/ppermute | solution.py:12
  1151.6 23.5 %collective-permute-done = bf16[16,65536]{1,0:T(8,128)(2,1)} collective-permute-done((bf16[16,65536]{1,0:T(8,128)(2,1)S(1)}, bf16[16,65536]{1,0:T(8,128)(2,1)}, u32[]{:S(2)}, u32[]{:S(2)}) %collective-permute-start) | collective-permute-done | bytes 2097184 | tf_op jit(solution)/shard_map/while/body/eval_jaxpr/ppermute | solution.py:12
  1182.4 23.5 %collective-permute-done = bf16[16,65536]{1,0:T(8,128)(2,1)} collective-permute-done((bf16[16,65536]{1,0:T(8,128)(2,1)S(1)}, bf16[16,65536]{1,0:T(8,128)(2,1)}, u32[]{:S(2)}, u32[]{:S(2)}) %collective-permute-start) | collective-permute-done | bytes 2097184 | tf_op jit(solution)/shard_map/while/body/eval_jaxpr/ppermute | solution.py:12
  1213.1 23.5 %collective-permute-done = bf16[16,65536]{1,0:T(8,128)(2,1)} collective-permute-done((bf16[16,65536]{1,0:T(8,128)(2,1)S(1)}, bf16[16,65536]{1,0:T(8,128)(2,1)}, u32[]{:S(2)}, u32[]{:S(2)}) %collective-permute-start) | collective-permute-done | bytes 2097184 | tf_op jit(solution)/shard_map/while/body/eval_jaxpr/ppermute | solution.py:12
  1237.0 10.9 fusion.18
  (78 shorter events, 173.6 us)
Async XLA Ops:
  6.5 458.4 %copy-start = (bf16[16,1,64,128]{3,2,1,0:T(8,128)(2,1)S(1)}, bf16[16,1,64,128]{3,2,1,0:T(8,128)(2,1)}, u32[]{:S(2)}) copy-start(bf16[16,1,64,128]{3,2,1,0:T(8,128)(2,1)} %param.10) | copy-start | bytes 786436
  229.8 228.8 %all-to-all-start = ((bf16[8,2,131072]{2,1,0:T(2,128)(2,1)}), bf16[8,2,131072]{2,1,0:T(2,128)(2,1)}, u32[]{:S(2)}, u32[]{:S(2)}) async-start(bf16[8,2,131072]{2,1,0:T(2,128)(2,1)} %reshape.136), calls=%async_computation | async-start | bytes 8388608 | tf_op jit(solution)/shard_map/all_to_all | solution.py:64
  458.7 6.3 copy-start.3
  458.7 6.7 copy-start.2
  458.7 8.0 copy-start.4
  458.7 152.2 %all-to-all-start.1 = ((bf16[8,2,262144]{2,1,0:T(2,128)(2,1)}), bf16[8,2,262144]{2,1,0:T(2,128)(2,1)}, u32[]{:S(2)}, u32[]{:S(2)}) async-start(bf16[8,2,262144]{2,1,0:T(2,128)(2,1)} %reshape.134), calls=%async_computation.1 | async-start | bytes 16777216 | tf_op jit(solution)/shard_map/all_to_all | solution.py:63
  464.5 134.5 %all-gather.2.cloned.1.call-start = ((), (), s32[]{:S(2)}) async-start(), calls=%async_computation.2 | async-start | bytes 2359296 | tf_op jit(solution)/shard_map/all_gather | solution.py:67
  776.7 29.2 %collective-permute-start = (bf16[16,65536]{1,0:T(8,128)(2,1)S(1)}, bf16[16,65536]{1,0:T(8,128)(2,1)}, u32[]{:S(2)}, u32[]{:S(2)}) collective-permute-start(bf16[16,65536]{1,0:T(8,128)(2,1)S(1)} %copy.66), channel_id=1, source_target_pairs={{120,0},{0,8},{8,16},{16,24},{24,32},{32,40},{40,48},{48,56},{56,6... | collective-permute-start | bytes 6291464 | tf_op jit(solution)/shard_map/while/body/eval_jaxpr/ppermute | solution.py:12
  807.5 29.2 %collective-permute-start = (bf16[16,65536]{1,0:T(8,128)(2,1)S(1)}, bf16[16,65536]{1,0:T(8,128)(2,1)}, u32[]{:S(2)}, u32[]{:S(2)}) collective-permute-start(bf16[16,65536]{1,0:T(8,128)(2,1)S(1)} %copy.66), channel_id=1, source_target_pairs={{120,0},{0,8},{8,16},{16,24},{24,32},{32,40},{40,48},{48,56},{56,6... | collective-permute-start | bytes 6291464 | tf_op jit(solution)/shard_map/while/body/eval_jaxpr/ppermute | solution.py:12
  838.2 29.2 %collective-permute-start = (bf16[16,65536]{1,0:T(8,128)(2,1)S(1)}, bf16[16,65536]{1,0:T(8,128)(2,1)}, u32[]{:S(2)}, u32[]{:S(2)}) collective-permute-start(bf16[16,65536]{1,0:T(8,128)(2,1)S(1)} %copy.66), channel_id=1, source_target_pairs={{120,0},{0,8},{8,16},{16,24},{24,32},{32,40},{40,48},{48,56},{56,6... | collective-permute-start | bytes 6291464 | tf_op jit(solution)/shard_map/while/body/eval_jaxpr/ppermute | solution.py:12
  869.0 29.2 %collective-permute-start = (bf16[16,65536]{1,0:T(8,128)(2,1)S(1)}, bf16[16,65536]{1,0:T(8,128)(2,1)}, u32[]{:S(2)}, u32[]{:S(2)}) collective-permute-start(bf16[16,65536]{1,0:T(8,128)(2,1)S(1)} %copy.66), channel_id=1, source_target_pairs={{120,0},{0,8},{8,16},{16,24},{24,32},{32,40},{40,48},{48,56},{56,6... | collective-permute-start | bytes 6291464 | tf_op jit(solution)/shard_map/while/body/eval_jaxpr/ppermute | solution.py:12
  899.8 29.2 %collective-permute-start = (bf16[16,65536]{1,0:T(8,128)(2,1)S(1)}, bf16[16,65536]{1,0:T(8,128)(2,1)}, u32[]{:S(2)}, u32[]{:S(2)}) collective-permute-start(bf16[16,65536]{1,0:T(8,128)(2,1)S(1)} %copy.66), channel_id=1, source_target_pairs={{120,0},{0,8},{8,16},{16,24},{24,32},{32,40},{40,48},{48,56},{56,6... | collective-permute-start | bytes 6291464 | tf_op jit(solution)/shard_map/while/body/eval_jaxpr/ppermute | solution.py:12
  930.5 29.2 %collective-permute-start = (bf16[16,65536]{1,0:T(8,128)(2,1)S(1)}, bf16[16,65536]{1,0:T(8,128)(2,1)}, u32[]{:S(2)}, u32[]{:S(2)}) collective-permute-start(bf16[16,65536]{1,0:T(8,128)(2,1)S(1)} %copy.66), channel_id=1, source_target_pairs={{120,0},{0,8},{8,16},{16,24},{24,32},{32,40},{40,48},{48,56},{56,6... | collective-permute-start | bytes 6291464 | tf_op jit(solution)/shard_map/while/body/eval_jaxpr/ppermute | solution.py:12
  961.3 29.2 %collective-permute-start = (bf16[16,65536]{1,0:T(8,128)(2,1)S(1)}, bf16[16,65536]{1,0:T(8,128)(2,1)}, u32[]{:S(2)}, u32[]{:S(2)}) collective-permute-start(bf16[16,65536]{1,0:T(8,128)(2,1)S(1)} %copy.66), channel_id=1, source_target_pairs={{120,0},{0,8},{8,16},{16,24},{24,32},{32,40},{40,48},{48,56},{56,6... | collective-permute-start | bytes 6291464 | tf_op jit(solution)/shard_map/while/body/eval_jaxpr/ppermute | solution.py:12
  992.1 29.2 %collective-permute-start = (bf16[16,65536]{1,0:T(8,128)(2,1)S(1)}, bf16[16,65536]{1,0:T(8,128)(2,1)}, u32[]{:S(2)}, u32[]{:S(2)}) collective-permute-start(bf16[16,65536]{1,0:T(8,128)(2,1)S(1)} %copy.66), channel_id=1, source_target_pairs={{120,0},{0,8},{8,16},{16,24},{24,32},{32,40},{40,48},{48,56},{56,6... | collective-permute-start | bytes 6291464 | tf_op jit(solution)/shard_map/while/body/eval_jaxpr/ppermute | solution.py:12
  1022.9 29.2 %collective-permute-start = (bf16[16,65536]{1,0:T(8,128)(2,1)S(1)}, bf16[16,65536]{1,0:T(8,128)(2,1)}, u32[]{:S(2)}, u32[]{:S(2)}) collective-permute-start(bf16[16,65536]{1,0:T(8,128)(2,1)S(1)} %copy.66), channel_id=1, source_target_pairs={{120,0},{0,8},{8,16},{16,24},{24,32},{32,40},{40,48},{48,56},{56,6... | collective-permute-start | bytes 6291464 | tf_op jit(solution)/shard_map/while/body/eval_jaxpr/ppermute | solution.py:12
  1053.6 29.2 %collective-permute-start = (bf16[16,65536]{1,0:T(8,128)(2,1)S(1)}, bf16[16,65536]{1,0:T(8,128)(2,1)}, u32[]{:S(2)}, u32[]{:S(2)}) collective-permute-start(bf16[16,65536]{1,0:T(8,128)(2,1)S(1)} %copy.66), channel_id=1, source_target_pairs={{120,0},{0,8},{8,16},{16,24},{24,32},{32,40},{40,48},{48,56},{56,6... | collective-permute-start | bytes 6291464 | tf_op jit(solution)/shard_map/while/body/eval_jaxpr/ppermute | solution.py:12
  1084.4 29.2 %collective-permute-start = (bf16[16,65536]{1,0:T(8,128)(2,1)S(1)}, bf16[16,65536]{1,0:T(8,128)(2,1)}, u32[]{:S(2)}, u32[]{:S(2)}) collective-permute-start(bf16[16,65536]{1,0:T(8,128)(2,1)S(1)} %copy.66), channel_id=1, source_target_pairs={{120,0},{0,8},{8,16},{16,24},{24,32},{32,40},{40,48},{48,56},{56,6... | collective-permute-start | bytes 6291464 | tf_op jit(solution)/shard_map/while/body/eval_jaxpr/ppermute | solution.py:12
  1115.2 29.2 %collective-permute-start = (bf16[16,65536]{1,0:T(8,128)(2,1)S(1)}, bf16[16,65536]{1,0:T(8,128)(2,1)}, u32[]{:S(2)}, u32[]{:S(2)}) collective-permute-start(bf16[16,65536]{1,0:T(8,128)(2,1)S(1)} %copy.66), channel_id=1, source_target_pairs={{120,0},{0,8},{8,16},{16,24},{24,32},{32,40},{40,48},{48,56},{56,6... | collective-permute-start | bytes 6291464 | tf_op jit(solution)/shard_map/while/body/eval_jaxpr/ppermute | solution.py:12
  1145.9 29.2 %collective-permute-start = (bf16[16,65536]{1,0:T(8,128)(2,1)S(1)}, bf16[16,65536]{1,0:T(8,128)(2,1)}, u32[]{:S(2)}, u32[]{:S(2)}) collective-permute-start(bf16[16,65536]{1,0:T(8,128)(2,1)S(1)} %copy.66), channel_id=1, source_target_pairs={{120,0},{0,8},{8,16},{16,24},{24,32},{32,40},{40,48},{48,56},{56,6... | collective-permute-start | bytes 6291464 | tf_op jit(solution)/shard_map/while/body/eval_jaxpr/ppermute | solution.py:12
  1176.7 29.2 %collective-permute-start = (bf16[16,65536]{1,0:T(8,128)(2,1)S(1)}, bf16[16,65536]{1,0:T(8,128)(2,1)}, u32[]{:S(2)}, u32[]{:S(2)}) collective-permute-start(bf16[16,65536]{1,0:T(8,128)(2,1)S(1)} %copy.66), channel_id=1, source_target_pairs={{120,0},{0,8},{8,16},{16,24},{24,32},{32,40},{40,48},{48,56},{56,6... | collective-permute-start | bytes 6291464 | tf_op jit(solution)/shard_map/while/body/eval_jaxpr/ppermute | solution.py:12
  1207.5 29.2 %collective-permute-start = (bf16[16,65536]{1,0:T(8,128)(2,1)S(1)}, bf16[16,65536]{1,0:T(8,128)(2,1)}, u32[]{:S(2)}, u32[]{:S(2)}) collective-permute-start(bf16[16,65536]{1,0:T(8,128)(2,1)S(1)} %copy.66), channel_id=1, source_target_pairs={{120,0},{0,8},{8,16},{16,24},{24,32},{32,40},{40,48},{48,56},{56,6... | collective-permute-start | bytes 6291464 | tf_op jit(solution)/shard_map/while/body/eval_jaxpr/ppermute | solution.py:12
  1236.9 13.2 %copy-start.1 = (bf16[16,1,64,128]{3,2,1,0:T(8,128)(2,1)S(1)}, bf16[16,1,64,128]{3,2,1,0:T(8,128)(2,1)}, u32[]{:S(2)}) copy-start(bf16[16,1,64,128]{3,2,1,0:T(8,128)(2,1)} %param.10) | copy-start | bytes 786436
Sparse Core Ops, SparseCore 0:
  467.0 131.9 all-gather.1
where the time goes:
time: 1270 us; the launch traced here: 1260 us
  other arithmetic  391 us (31%)
  waiting for transfers between devices  363 us (29%)
  local copies, waits for them, and re-layouts  359 us (28%)
  matrix products  118 us (9%)
  between operations  14.1 us (1%)
    unnamed x2, other arithmetic  358 us
    ppermute x15, waiting for transfers between devices, passed_along(): return lax.ppermute(block, axis, route)  353 us
    unnamed x21, local copies, waits for them, and re-layouts  143 us
    dot_general x16, matrix products, place_tile(): jnp.einsum('dk,qk->dq', documents, current, preferred_element_type=jnp.fl...  95.5 us
    gather x2, local copies, waits for them, and re-layouts, doc_gradients(): picked_grads = jnp.take(gradients, token_index, axis=2)  77.4 us
    gather x1, local copies, waits for them, and re-layouts, doc_gradients(): picked_acts = jnp.take(activations, token_index, axis=2) * inside  60.5 us
  transfers between devices with their start and end apart: 18, of which 16 were waited for; matrix products, arithmetic and copies ran while one was open for 35% of the time, Pallas kernels for 0%

commit v1 on v0

v1 whole, which is shorter than its diff:
```python
import functools

import jax
import jax.numpy as jnp
from jax import lax
from jax.experimental import pallas as pl
from jax.experimental.pallas import tpu as pltpu
from jax.sharding import PartitionSpec as P

F32, BF16 = jnp.float32, jnp.bfloat16
KA, KG, DOCS, TOK = 128, 64, 64, 4096
WIDTH = KA * KG
HALF = WIDTH // 2
ORDER = (0, 1, 2, 3, 6, 7, 4, 5)
NT = (((1,), (1,)), ((), ()))
DOC_PITCH = 72
QUERY_PITCH = 24


def from_partner(block, axis, mask):
    n = lax.axis_size(axis)
    return lax.ppermute(block, axis, [(i ^ mask, i) for i in range(n)])


def bf16_parts(x):
    first = x.astype(BF16)
    rest = x - first.astype(F32)
    second = rest.astype(BF16)
    third = (rest - second.astype(F32)).astype(BF16)
    return first, second, third


def panel_kernel(query_ref, ginv_ref, ainv_ref, out_ref, rows):
    count = query_ref.shape[0]
    queries = query_ref[...].reshape(count * KG, KA)
    right = sum(
        jnp.dot(queries, part, preferred_element_type=F32)
        for part in reversed(bf16_parts(ainv_ref[0]))
    )
    side_by_side = jnp.concatenate(
        [right[q * KG : (q + 1) * KG] for q in range(count)], axis=1
    )
    both = jnp.dot(
        ginv_ref[0], side_by_side, precision=lax.Precision.HIGHEST, preferred_element_type=F32
    )
    for q in range(count):
        rows[pl.ds(q, KG, stride=QUERY_PITCH), :] = both[:, q * KA : (q + 1) * KA]
    for g in range(KG):
        out_ref[:, g * KA : (g + 1) * KA] = rows[pl.ds(g * QUERY_PITCH, count), :].astype(BF16)


def panel(query_grads, ginv, ainv):
    count = query_grads.shape[0]
    return pl.pallas_call(
        panel_kernel,
        out_shape=jax.ShapeDtypeStruct((count, WIDTH), BF16),
        scratch_shapes=[pltpu.VMEM((KG * QUERY_PITCH, KA), F32)],
        compiler_params=pltpu.CompilerParams(vmem_limit_bytes=32 << 20),
        cost_estimate=pl.CostEstimate(flops=400_000_000, bytes_accessed=1 << 20, transcendentals=0),
        name="panel",
    )(query_grads.reshape(count, KG, KA), ginv, ainv)


def docs_kernel(at_ref, lengths_ref, act_ref, grad_ref, out_ref, rows):
    o = pl.program_id(0)
    lane = lax.broadcasted_iota(jnp.int32, (KG, 256), 1)

    def document(j, start):
        end = start + lengths_ref[o, j]
        base = pl.multiple_of(jnp.minimum(start >> 7, TOK // 128 - 2) * 128, 128)
        acts = act_ref[0, :, pl.ds(base, 256)]
        grads = grad_ref[0, :, pl.ds(base, 256)]
        inside = (lane >= start - base) & (lane < end - base)
        grads = jnp.where(inside, grads, jnp.zeros_like(grads))
        rows[pl.ds(j, KG, stride=DOC_PITCH), :] = lax.dot_general(
            grads, acts, NT, preferred_element_type=F32
        )
        return end

    lax.fori_loop(0, DOCS, document, jnp.int32(0), unroll=32)
    for g in range(KG):
        out_ref[:, g * KA : (g + 1) * KA] = rows[pl.ds(g * DOC_PITCH, DOCS), :].astype(BF16)


def doc_gradients(owner_at, lengths, act_rows, grad_rows):
    owners = lengths.shape[0]
    return pl.pallas_call(
        docs_kernel,
        grid_spec=pltpu.PrefetchScalarGridSpec(
            num_scalar_prefetch=2,
            grid=(owners,),
            in_specs=[
                pl.BlockSpec((1, KA, TOK), lambda o, at, n: (0, 0, at[o])),
                pl.BlockSpec((1, KG, TOK), lambda o, at, n: (0, 0, at[o])),
            ],
            out_specs=pl.BlockSpec((DOCS, WIDTH), lambda o, at, n: (o, 0)),
            scratch_shapes=[pltpu.VMEM((KG * DOC_PITCH, KA), F32)],
        ),
        out_shape=jax.ShapeDtypeStruct((owners * DOCS, WIDTH), BF16),
        compiler_params=pltpu.CompilerParams(vmem_limit_bytes=32 << 20),
        cost_estimate=pl.CostEstimate(
            flops=owners * 2_000_000_000, bytes_accessed=owners * 5 << 19, transcendentals=0
        ),
        name="docs",
    )(owner_at, lengths, act_rows, grad_rows)


K_BLOCK = 1024


def score_kernel(doc_ref, *refs):
    k = pl.program_id(0)
    *piece_refs, out_ref = refs
    pieces = [ref[...] for ref in piece_refs]
    halves = pieces[12:]
    low = k < HALF // K_BLOCK
    whole = pieces[:12] + [
        jnp.where(low, halves[2 * i], halves[2 * i + 1]) for i in range(len(halves) // 2)
    ]
    by_mask = dict(zip(WHOLE + SPLIT, whole))
    panels = jnp.concatenate([by_mask[m] for m in range(16)], axis=0)
    tile = lax.dot_general(doc_ref[...], panels, NT, preferred_element_type=F32)

    @pl.when(k == 0)
    def _():
        out_ref[...] = tile

    @pl.when(k > 0)
    def _():
        out_ref[...] += tile


WHOLE = (0, 2, 6, 8, 10, 14, 1, 3, 7, 9, 11, 15)
SPLIT = (4, 12, 5, 13)


def partial_scores(documents, whole, split):
    rows, count = documents.shape[0], whole[0].shape[0]
    half_steps = HALF // K_BLOCK
    in_specs = [pl.BlockSpec((rows, K_BLOCK), lambda k: (0, k))]
    in_specs += [pl.BlockSpec((count, K_BLOCK), lambda k: (0, k)) for _ in whole]
    flat = []
    for low, high in split:
        in_specs.append(pl.BlockSpec((count, K_BLOCK), lambda k: (0, jnp.minimum(k, half_steps - 1))))
        in_specs.append(pl.BlockSpec((count, K_BLOCK), lambda k: (0, jnp.maximum(k - half_steps, 0))))
        flat += [low, high]
    return pl.pallas_call(
        score_kernel,
        grid=(WIDTH // K_BLOCK,),
        in_specs=in_specs,
        out_specs=pl.BlockSpec((rows, 16 * count), lambda k: (0, 0)),
        out_shape=jax.ShapeDtypeStruct((rows, 16 * count), F32),
        compiler_params=pltpu.CompilerParams(vmem_limit_bytes=32 << 20),
        cost_estimate=pl.CostEstimate(
            flops=2 * rows * 16 * count * WIDTH, bytes_accessed=12 << 20, transcendentals=0
        ),
        name="scores",
    )(documents, *whole, *flat)


def place_kernel(blk_ref, mine_ref, theirs_ref, out_ref):
    x = mine_ref[...] + theirs_ref[...]
    lane = lax.broadcasted_iota(jnp.int32, x.shape, 1)
    width = x.shape[1]
    for bit in range(4):
        step = width // 16 << bit
        swapped = jnp.where(
            lane & step != 0, pltpu.roll(x, step, 1), pltpu.roll(x, width - step, 1)
        )
        x = jnp.where((blk_ref[0] >> bit) & 1 != 0, swapped, x)
    out_ref[...] = x


def place(blk, mine, theirs):
    vmem = pl.BlockSpec(memory_space=pltpu.VMEM)
    return pl.pallas_call(
        place_kernel,
        in_specs=[pl.BlockSpec(memory_space=pltpu.SMEM), vmem, vmem],
        out_specs=vmem,
        out_shape=jax.ShapeDtypeStruct(mine.shape, F32),
        name="place",
    )(blk, mine, theirs)


def local(act_rows, grad_rows, query_grads, ginv, ainv, lengths):
    blk, tp = lax.axis_index("blk"), lax.axis_index("tp")

    for mask in (1, 2, 6):
        lengths = jnp.concatenate([lengths, from_partner(lengths, "tp", mask)], axis=0)
    owner_at = jnp.int32(tp) ^ jnp.asarray(ORDER, jnp.int32)

    own = panel(query_grads, ginv, ainv)

    def take(block, mask):
        return from_partner(block, "blk", mask)

    got, halves = {0: own}, {}
    got[8] = take(own, 8)
    got[2], got[6] = take(own, 2), take(own, 6)
    for z in (0, 8):
        if z:
            got[z | 2], got[z | 6] = take(got[z], 2), take(got[z], 6)
        halves[z | 4] = (
            take(got[z | 6][:, :HALF], 2),
            take(got[z | 2][:, HALF:], 6),
        )
    for mask in list(got):
        got[mask | 1] = take(got[mask], 1)
    for mask in list(halves):
        halves[mask | 1] = tuple(take(part, 1) for part in halves[mask])

    documents = doc_gradients(owner_at, lengths, act_rows, grad_rows)
    scores = partial_scores(documents, [got[m] for m in WHOLE], [halves[m] for m in SPLIT])

    for mask in (6, 2):
        rows = scores.shape[0] // 2
        scores = scores[:rows] + from_partner(scores[rows:], "tp", mask)
    rows = scores.shape[0] // 2
    theirs = from_partner(scores[rows:], "tp", 1)
    return place(jnp.int32(blk).reshape(1), scores[:rows], theirs)


def solution(mesh):
    placed = (
        P("tp", None, "blk"),
        P("tp", None, "blk"),
        P("blk", "tp", None, None),
        P("tp", None, None),
        P("tp", None, None),
        P(("blk", "tp"), None),
    )
    return jax.shard_map(
        local, mesh=mesh, in_specs=placed, out_specs=P(("blk", "tp"), None), check_vma=False
    )
```

time: 1270 us -> 92.1 us (0.07)
  other arithmetic: 391 us -> 2.7 us
  local copies, waits for them, and re-layouts: 359 us -> 9.43 us
  waiting for transfers between devices: 363 us -> 26.8 us
  matrix products: 118 us -> 0 us
  Pallas kernels: 0 us -> 25.1 us
  starting transfers between devices: 12.5 us -> 27.5 us
  between operations: 14.1 us -> 0.15 us
    unnamed x2 -> x0, other arithmetic: 358 us -> none
    ppermute x15 -> x25, waiting for transfers between devices: 353 us -> 26.8 us  [from_partner(): return lax.ppermute(block, axis, [(i ^ mask, i) for i in range(n)])]
    gather x3 -> x0, local copies, waits for them, and re-layouts: 138 us -> none  [the longest x2 77.4 us: doc_gradients(): picked_grads = jnp.take(gradients, token_index, axis=2)]
    unnamed x21 -> x12, local copies, waits for them, and re-layouts: 143 us -> 8.73 us
    dot_general x19 -> x0, matrix products: 118 us -> none  [the longest x16 95.5 us: place_tile(): jnp.einsum('dk,qk->dq', documents, current, preferred_element_type=jnp.fl...]
    all_to_all x2 -> x0, local copies, waits for them, and re-layouts: 50.3 us -> none  [the longest x1 25.1 us: local(): lax.all_to_all(act_rows, 'tp', split_axis=2, concat_axis=0, tiled=True)]
    ppermute x15 -> x25, starting transfers between devices: 0.04 us -> 27.5 us  [from_partner(): return lax.ppermute(block, axis, [(i ^ mask, i) for i in range(n)])]
    pallas_call x0 -> x4, Pallas kernels: none -> 25.1 us  [the longest x1 16.1 us: doc_gradients(): pl.pallas_call(docs_kernel, grid_spec=pltpu.PrefetchScalarGridSpec(num_sc...]
  transfers between devices with their start and end apart: 18 -> 25, of which waited for: 16 -> 9; matrix products, arithmetic and copies ran while one was open for 35% -> 3% of each run, Pallas kernels for 0% -> 18%
where the time goes in v1:
time: 92.1 us; the launch traced here: 91.7 us
  starting transfers between devices  27.5 us (30%)
  waiting for transfers between devices  26.8 us (29%)
  Pallas kernels  25.1 us (27%)
  local copies, waits for them, and re-layouts  9.43 us (10%)
  other arithmetic  2.7 us (3%)
    ppermute x25, starting transfers between devices, from_partner(): return lax.ppermute(block, axis, [(i ^ mask, i) for i in range(n)])  27.5 us
    ppermute x25, waiting for transfers between devices, from_partner(): return lax.ppermute(block, axis, [(i ^ mask, i) for i in range(n)])  26.8 us
    pallas_call x1, Pallas kernels, doc_gradients(): pl.pallas_call(docs_kernel, grid_spec=pltpu.PrefetchScalarGridSpec(num_sc...  16.1 us
    unnamed x12, local copies, waits for them, and re-layouts  8.73 us
    pallas_call x1, Pallas kernels, partial_scores(): pl.pallas_call(score_kernel, grid=(WIDTH // K_BLOCK,), in_specs=in_specs,...  6 us
    concatenate x3, other arithmetic, local(): jnp.concatenate([lengths, from_partner(lengths, 'tp', mask)], axis=0)  1.99 us
  transfers between devices with their start and end apart: 25, of which 9 were waited for; matrix products, arithmetic and copies ran while one was open for 3% of the time, Pallas kernels for 18%

profile of v1, /device:TPU:0, one launch (start us, length us, event | category | flops | bytes accessed | tf_op | source)
XLA Modules:
  0.0 91.7 jit_solution(15059906557293292815)
XLA Ops:
  0.0 0.9 %copy-done.2 = bf16[16,1,64,128]{3,2,1,0:T(8,128)(2,1)S(1)} copy-done((bf16[16,1,64,128]{3,2,1,0:T(8,128)(2,1)S(1)}, bf16[16,1,64,128]{3,2,1,0:T(8,128)(2,1)}, u32[]{:S(2)}) %copy-start.2) | copy-done | bytes 262168
  1.0 0.8 copy-done.3
  1.8 0.8 copy-done.4
  2.5 1.2 %panel.1.refs_0_ = bf16[16,8192]{1,0:T(8,128)(2,1)S(1)} custom-call(bf16[16,64,128]{2,1,0:T(8,128)(2,1)S(1)} %bitcast.2, f32[1,64,64]{2,1,0:T(8,128)S(1)} %copy-done.4, f32[1,128,128]{2,1,0:T(8,128)S(1)} %copy-done.3), custom_call_target="tpu_custom_call" | custom-call | flops 400000000 | bytes 1048576 | tf_op jit(solution)/shard_map/panel/pallas_call | solution.py:54
  3.7 4.0 %collective-permute-start.5 = (bf16[16,8192]{1,0:T(8,128)(2,1)S(1)}, bf16[16,8192]{1,0:T(8,128)(2,1)S(1)}, u32[]{:S(2)}, u32[]{:S(2)}) collective-permute-start(bf16[16,8192]{1,0:T(8,128)(2,1)S(1)} %panel.1.refs_0_), channel_id=1, source_target_pairs={{64,0},{72,8},{80,16},{88,24},{96,32},{104,40},{112,48},{120,56},{... | collective-permute-start | bytes 786440 | tf_op jit(solution)/shard_map/ppermute | solution.py:22
  7.8 2.8 %collective-permute-start.4 = (bf16[16,8192]{1,0:T(8,128)(2,1)S(1)}, bf16[16,8192]{1,0:T(8,128)(2,1)S(1)}, u32[]{:S(2)}, u32[]{:S(2)}) collective-permute-start(bf16[16,8192]{1,0:T(8,128)(2,1)S(1)} %panel.1.refs_0_), channel_id=1, source_target_pairs={{48,0},{56,8},{32,16},{40,24},{16,32},{24,40},{0,48},{8,56},{112,6... | collective-permute-start | bytes 786440 | tf_op jit(solution)/shard_map/ppermute | solution.py:22
  10.7 3.3 %collective-permute-done.5.refs_3_ = bf16[16,8192]{1,0:T(8,128)(2,1)S(1)} collective-permute-done((bf16[16,8192]{1,0:T(8,128)(2,1)S(1)}, bf16[16,8192]{1,0:T(8,128)(2,1)S(1)}, u32[]{:S(2)}, u32[]{:S(2)}) %collective-permute-start.5) | collective-permute-done | bytes 262176 | tf_op jit(solution)/shard_map/ppermute | solution.py:22
  14.1 2.8 %collective-permute-start.7 = (bf16[16,8192]{1,0:T(8,128)(2,1)S(1)}, bf16[16,8192]{1,0:T(8,128)(2,1)S(1)}, u32[]{:S(2)}, u32[]{:S(2)}) collective-permute-start(bf16[16,8192]{1,0:T(8,128)(2,1)S(1)} %collective-permute-done.5.refs_3_), channel_id=1, source_target_pairs={{48,0},{56,8},{32,16},{40,24},{16,32},{24,40},{0,48},{8,56},{112,6... | collective-permute-start | bytes 786440 | tf_op jit(solution)/shard_map/ppermute | solution.py:22
  17.1 1.3 %collective-permute-start = (s32[1,64]{1,0:T(1,128)}, s32[1,64]{1,0:T(1,128)S(1)}, u32[]{:S(2)}, u32[]{:S(2)}) collective-permute-start(s32[1,64]{1,0:T(1,128)} %param.12), channel_id=1, source_target_pairs={{1,0},{0,1},{3,2},{2,3},{5,4},{4,5},{7,6},{6,7},{9,8},{8,9},{11,10... | collective-permute-start | bytes 776 | tf_op jit(solution)/shard_map/ppermute | solution.py:22
  18.3 2.4 %collective-permute-done = s32[1,64]{1,0:T(1,128)S(1)} collective-permute-done((s32[1,64]{1,0:T(1,128)}, s32[1,64]{1,0:T(1,128)S(1)}, u32[]{:S(2)}, u32[]{:S(2)}) %collective-permute-start) | collective-permute-done | bytes 288 | tf_op jit(solution)/shard_map/ppermute | solution.py:22
  21.2 0.7 pad_add_fusion.2
  21.9 1.7 %collective-permute-start.1 = (s32[2,64]{1,0:T(2,128)S(1)}, s32[2,64]{1,0:T(2,128)S(1)}, u32[]{:S(2)}, u32[]{:S(2)}) collective-permute-start(s32[2,64]{1,0:T(2,128)S(1)} %pad_add_fusion.2), channel_id=1, source_target_pairs={{2,0},{3,1},{0,2},{1,3},{6,4},{7,5},{4,6},{5,7},{10,8},{11,9},{8,1... | collective-permute-start | bytes 1544 | tf_op jit(solution)/shard_map/ppermute | solution.py:22
  23.6 2.0 %collective-permute-done.1 = s32[2,64]{1,0:T(2,128)S(1)} collective-permute-done((s32[2,64]{1,0:T(2,128)S(1)}, s32[2,64]{1,0:T(2,128)S(1)}, u32[]{:S(2)}, u32[]{:S(2)}) %collective-permute-start.1) | collective-permute-done | bytes 544 | tf_op jit(solution)/shard_map/ppermute | solution.py:22
  25.6 1.8 %collective-permute-start.14 = (bf16[16,4096]{1,0:T(8,128)(2,1)S(1)}, bf16[16,4096]{1,0:T(8,128)(2,1)S(1)}, u32[]{:S(2)}, u32[]{:S(2)}) collective-permute-start(bf16[16,4096]{1,0:T(8,128)(2,1)S(1)} %slice.40), channel_id=1, source_target_pairs={{16,0},{24,8},{0,16},{8,24},{48,32},{56,40},{32,48},{40,56},{80,64... | collective-permute-start | bytes 393224 | tf_op jit(solution)/shard_map/ppermute | solution.py:22
  27.8 0.7 pad_add_fusion.1
  28.5 3.1 %collective-permute-start.2 = (s32[4,64]{1,0:T(4,128)S(1)}, s32[4,64]{1,0:T(4,128)S(1)}, u32[]{:S(2)}, u32[]{:S(2)}) collective-permute-start(s32[4,64]{1,0:T(4,128)S(1)} %pad_add_fusion.1), channel_id=1, source_target_pairs={{6,0},{7,1},{4,2},{5,3},{2,4},{3,5},{0,6},{1,7},{14,8},{15,9},{12,... | collective-permute-start | bytes 3080 | tf_op jit(solution)/shard_map/ppermute | solution.py:22
  31.6 1.7 %collective-permute-done.2 = s32[4,64]{1,0:T(4,128)S(1)} collective-permute-done((s32[4,64]{1,0:T(4,128)S(1)}, s32[4,64]{1,0:T(4,128)S(1)}, u32[]{:S(2)}, u32[]{:S(2)}) %collective-permute-start.2) | collective-permute-done | bytes 1056 | tf_op jit(solution)/shard_map/ppermute | solution.py:22
  34.3 2.6 %collective-permute-start.17 = (bf16[16,4096]{1,0:T(8,128)(2,1)S(1)}, bf16[16,4096]{1,0:T(8,128)(2,1)S(1)}, u32[]{:S(2)}, u32[]{:S(2)}) collective-permute-start(bf16[16,4096]{1,0:T(8,128)(2,1)S(1)} %slice.43), channel_id=1, source_target_pairs={{48,0},{56,8},{32,16},{40,24},{16,32},{24,40},{0,48},{8,56},{112,6... | collective-permute-start | bytes 393224 | tf_op jit(solution)/shard_map/ppermute | solution.py:22
  36.9 0.7 broadcast_xor_fusion.at_ref
  37.5 0.7 pad_add_fusion.lengths_ref
  38.9 0.9 collective-permute-done.16.refs_14_
  39.8 1.3 %collective-permute-done.17.refs_15_ = bf16[16,4096]{1,0:T(8,128)(2,1)S(1)} collective-permute-done((bf16[16,4096]{1,0:T(8,128)(2,1)S(1)}, bf16[16,4096]{1,0:T(8,128)(2,1)S(1)}, u32[]{:S(2)}, u32[]{:S(2)}) %collective-permute-start.17) | collective-permute-done | bytes 131104 | tf_op jit(solution)/shard_map/ppermute | solution.py:22
  41.1 3.4 %copy-done = bf16[1,128,32768]{2,1,0:T(8,128)(2,1)S(1)} copy-done((bf16[1,128,32768]{2,1,0:T(8,128)(2,1)S(1)}, bf16[1,128,32768]{2,1,0:T(8,128)(2,1)}, u32[]{:S(2)}) %copy-start) | copy-done | bytes 8388632
  44.5 2.2 %copy-done.1 = bf16[1,64,32768]{2,1,0:T(8,128)(2,1)S(1)} copy-done((bf16[1,64,32768]{2,1,0:T(8,128)(2,1)S(1)}, bf16[1,64,32768]{2,1,0:T(8,128)(2,1)}, u32[]{:S(2)}) %copy-start.1) | copy-done | bytes 4194328
  46.7 16.1 %docs.1.doc_ref = bf16[512,8192]{1,0:T(8,128)(2,1)S(1)} custom-call(s32[8]{0:T(128)S(1)} %broadcast_xor_fusion.at_ref, s32[8,64]{1,0:T(8,128)S(1)} %pad_add_fusion.lengths_ref, bf16[1,128,32768]{2,1,0:T(8,128)(2,1)S(1)} %copy-done, bf16[1,64,32768]{2,1,0:T(8,128)(2,1)S(1)} %copy-done.1), custom_call_target="tpu_custom_call" | custom-call | flops 16000000000 | bytes 20971520 | tf_op jit(solution)/shard_map/docs/pallas_call | solution.py:87
  62.9 6.0 %scores.1 = f32[512,256]{1,0:T(8,128)S(1)} custom-call(bf16[512,8192]{1,0:T(8,128)(2,1)S(1)} %docs.1.doc_ref, bf16[16,8192]{1,0:T(8,128)(2,1)S(1)} %panel.1.refs_0_, bf16[16,8192]{1,0:T(8,128)(2,1)S(1)} %collective-permute-done.3.refs_1_, bf16[16,8192]{1,0:T(8,128)(2,1)S(1)} %collective-permute-done.4.refs_2_, ...), custom_call_target="tpu_custom_call" | custom-call | flops 2147483648 | bytes 12582912 | tf_op jit(solution)/shard_map/scores/pallas_call | solution.py:147
  68.9 3.1 %collective-permute-start.22 = (f32[256,256]{1,0:T(8,128)S(1)}, f32[256,256]{1,0:T(8,128)S(1)}, u32[]{:S(2)}, u32[]{:S(2)}) collective-permute-start(f32[256,256]{1,0:T(8,128)S(1)} %slice.45), channel_id=1, source_target_pairs={{6,0},{7,1},{4,2},{5,3},{2,4},{3,5},{0,6},{1,7},{14,8},{15,9},{12,... | collective-permute-start | bytes 786440 | tf_op jit(solution)/shard_map/ppermute | solution.py:22
  72.0 7.0 %collective-permute-done.22 = f32[256,256]{1,0:T(8,128)S(1)} collective-permute-done((f32[256,256]{1,0:T(8,128)S(1)}, f32[256,256]{1,0:T(8,128)S(1)}, u32[]{:S(2)}, u32[]{:S(2)}) %collective-permute-start.22) | collective-permute-done | bytes 262176 | tf_op jit(solution)/shard_map/ppermute | solution.py:22
  79.1 5.2 %collective-permute-done.23 = f32[128,256]{1,0:T(8,128)S(1)} collective-permute-done((f32[128,256]{1,0:T(8,128)S(1)}, f32[128,256]{1,0:T(8,128)S(1)}, u32[]{:S(2)}, u32[]{:S(2)}) %collective-permute-start.23) | collective-permute-done | bytes 131104 | tf_op jit(solution)/shard_map/ppermute | solution.py:22
  85.0 1.3 %collective-permute-start.24 = (f32[64,256]{1,0:T(8,128)S(1)}, f32[64,256]{1,0:T(8,128)S(1)}, u32[]{:S(2)}, u32[]{:S(2)}) collective-permute-start(f32[64,256]{1,0:T(8,128)S(1)} %get-tuple-element.5), channel_id=1, source_target_pairs={{1,0},{0,1},{3,2},{2,3},{5,4},{4,5},{7,6},{6,7},{9,8},{8,9},{11,10... | collective-permute-start | bytes 196616 | tf_op jit(solution)/shard_map/ppermute | solution.py:22
  86.3 3.0 %collective-permute-done.24.theirs_ref = f32[64,256]{1,0:T(8,128)S(1)} collective-permute-done((f32[64,256]{1,0:T(8,128)S(1)}, f32[64,256]{1,0:T(8,128)S(1)}, u32[]{:S(2)}, u32[]{:S(2)}) %collective-permute-start.24) | collective-permute-done | bytes 65568 | tf_op jit(solution)/shard_map/ppermute | solution.py:22
  89.9 1.8 %place.1 = f32[64,256]{1,0:T(8,128)} custom-call(s32[1]{0:T(128)} %bitcast.blk_ref, f32[64,256]{1,0:T(8,128)} %get-tuple-element.6.mine_ref, f32[64,256]{1,0:T(8,128)} %copy-done.5), custom_call_target="tpu_custom_call" | custom-call | tf_op jit(solution)/shard_map/place/pallas_call | solution.py:176
  (47 shorter events, 4.6 us)
Async XLA Ops:
  0.0 0.9 %copy-start.2 = (bf16[16,1,64,128]{3,2,1,0:T(8,128)(2,1)S(1)}, bf16[16,1,64,128]{3,2,1,0:T(8,128)(2,1)}, u32[]{:S(2)}) copy-start(bf16[16,1,64,128]{3,2,1,0:T(8,128)(2,1)} %param.9) | copy-start | bytes 786436
  1.0 0.8 copy-start.3
  1.8 0.8 copy-start.4
  3.7 10.3 %collective-permute-start.5 = (bf16[16,8192]{1,0:T(8,128)(2,1)S(1)}, bf16[16,8192]{1,0:T(8,128)(2,1)S(1)}, u32[]{:S(2)}, u32[]{:S(2)}) collective-permute-start(bf16[16,8192]{1,0:T(8,128)(2,1)S(1)} %panel.1.refs_0_), channel_id=1, source_target_pairs={{64,0},{72,8},{80,16},{88,24},{96,32},{104,40},{112,48},{120,56},{... | collective-permute-start | bytes 786440 | tf_op jit(solution)/shard_map/ppermute | solution.py:22
  7.8 13.0 %collective-permute-start.4 = (bf16[16,8192]{1,0:T(8,128)(2,1)S(1)}, bf16[16,8192]{1,0:T(8,128)(2,1)S(1)}, u32[]{:S(2)}, u32[]{:S(2)}) collective-permute-start(bf16[16,8192]{1,0:T(8,128)(2,1)S(1)} %panel.1.refs_0_), channel_id=1, source_target_pairs={{48,0},{56,8},{32,16},{40,24},{16,32},{24,40},{0,48},{8,56},{112,6... | collective-permute-start | bytes 786440 | tf_op jit(solution)/shard_map/ppermute | solution.py:22
  10.5 11.4 %collective-permute-start.3 = (bf16[16,8192]{1,0:T(8,128)(2,1)S(1)}, bf16[16,8192]{1,0:T(8,128)(2,1)S(1)}, u32[]{:S(2)}, u32[]{:S(2)}) collective-permute-start(bf16[16,8192]{1,0:T(8,128)(2,1)S(1)} %panel.1.refs_0_), channel_id=1, source_target_pairs={{16,0},{24,8},{0,16},{8,24},{48,32},{56,40},{32,48},{40,56},{80,64... | collective-permute-start | bytes 786440 | tf_op jit(solution)/shard_map/ppermute | solution.py:22
  14.1 13.3 %collective-permute-start.7 = (bf16[16,8192]{1,0:T(8,128)(2,1)S(1)}, bf16[16,8192]{1,0:T(8,128)(2,1)S(1)}, u32[]{:S(2)}, u32[]{:S(2)}) collective-permute-start(bf16[16,8192]{1,0:T(8,128)(2,1)S(1)} %collective-permute-done.5.refs_3_), channel_id=1, source_target_pairs={{48,0},{56,8},{32,16},{40,24},{16,32},{24,40},{0,48},{8,56},{112,6... | collective-permute-start | bytes 786440 | tf_op jit(solution)/shard_map/ppermute | solution.py:22
  16.8 11.7 %collective-permute-start.6 = (bf16[16,8192]{1,0:T(8,128)(2,1)S(1)}, bf16[16,8192]{1,0:T(8,128)(2,1)S(1)}, u32[]{:S(2)}, u32[]{:S(2)}) collective-permute-start(bf16[16,8192]{1,0:T(8,128)(2,1)S(1)} %collective-permute-done.5.refs_3_), channel_id=1, source_target_pairs={{16,0},{24,8},{0,16},{8,24},{48,32},{56,40},{32,48},{40,56},{80,64... | collective-permute-start | bytes 786440 | tf_op jit(solution)/shard_map/ppermute | solution.py:22
  17.1 3.7 %collective-permute-start = (s32[1,64]{1,0:T(1,128)}, s32[1,64]{1,0:T(1,128)S(1)}, u32[]{:S(2)}, u32[]{:S(2)}) collective-permute-start(s32[1,64]{1,0:T(1,128)} %param.12), channel_id=1, source_target_pairs={{1,0},{0,1},{3,2},{2,3},{5,4},{4,5},{7,6},{6,7},{9,8},{8,9},{11,10... | collective-permute-start | bytes 776 | tf_op jit(solution)/shard_map/ppermute | solution.py:22
  20.7 13.3 %collective-permute-start.8 = (bf16[16,8192]{1,0:T(8,128)(2,1)S(1)}, bf16[16,8192]{1,0:T(8,128)(2,1)S(1)}, u32[]{:S(2)}, u32[]{:S(2)}) collective-permute-start(bf16[16,8192]{1,0:T(8,128)(2,1)S(1)} %panel.1.refs_0_), channel_id=1, source_target_pairs={{8,0},{0,8},{24,16},{16,24},{40,32},{32,40},{56,48},{48,56},{72,64... | collective-permute-start | bytes 786440 | tf_op jit(solution)/shard_map/ppermute | solution.py:22
  20.7 13.5 %collective-permute-start.11 = (bf16[16,8192]{1,0:T(8,128)(2,1)S(1)}, bf16[16,8192]{1,0:T(8,128)(2,1)S(1)}, u32[]{:S(2)}, u32[]{:S(2)}) collective-permute-start(bf16[16,8192]{1,0:T(8,128)(2,1)S(1)} %collective-permute-done.5.refs_3_), channel_id=1, source_target_pairs={{8,0},{0,8},{24,16},{16,24},{40,32},{32,40},{56,48},{48,56},{72,64... | collective-permute-start | bytes 786440 | tf_op jit(solution)/shard_map/ppermute | solution.py:22
  21.9 3.6 %collective-permute-start.1 = (s32[2,64]{1,0:T(2,128)S(1)}, s32[2,64]{1,0:T(2,128)S(1)}, u32[]{:S(2)}, u32[]{:S(2)}) collective-permute-start(s32[2,64]{1,0:T(2,128)S(1)} %pad_add_fusion.2), channel_id=1, source_target_pairs={{2,0},{3,1},{0,2},{1,3},{6,4},{7,5},{4,6},{5,7},{10,8},{11,9},{8,1... | collective-permute-start | bytes 1544 | tf_op jit(solution)/shard_map/ppermute | solution.py:22
  25.6 7.8 %collective-permute-start.14 = (bf16[16,4096]{1,0:T(8,128)(2,1)S(1)}, bf16[16,4096]{1,0:T(8,128)(2,1)S(1)}, u32[]{:S(2)}, u32[]{:S(2)}) collective-permute-start(bf16[16,4096]{1,0:T(8,128)(2,1)S(1)} %slice.40), channel_id=1, source_target_pairs={{16,0},{24,8},{0,16},{8,24},{48,32},{56,40},{32,48},{40,56},{80,64... | collective-permute-start | bytes 393224 | tf_op jit(solution)/shard_map/ppermute | solution.py:22
  27.4 6.5 %collective-permute-start.15 = (bf16[16,4096]{1,0:T(8,128)(2,1)S(1)}, bf16[16,4096]{1,0:T(8,128)(2,1)S(1)}, u32[]{:S(2)}, u32[]{:S(2)}) collective-permute-start(bf16[16,4096]{1,0:T(8,128)(2,1)S(1)} %slice.41), channel_id=1, source_target_pairs={{48,0},{56,8},{32,16},{40,24},{16,32},{24,40},{0,48},{8,56},{112,6... | collective-permute-start | bytes 393224 | tf_op jit(solution)/shard_map/ppermute | solution.py:22
  28.5 4.9 %collective-permute-start.2 = (s32[4,64]{1,0:T(4,128)S(1)}, s32[4,64]{1,0:T(4,128)S(1)}, u32[]{:S(2)}, u32[]{:S(2)}) collective-permute-start(s32[4,64]{1,0:T(4,128)S(1)} %pad_add_fusion.1), channel_id=1, source_target_pairs={{6,0},{7,1},{4,2},{5,3},{2,4},{3,5},{0,6},{1,7},{14,8},{15,9},{12,... | collective-permute-start | bytes 3080 | tf_op jit(solution)/shard_map/ppermute | solution.py:22
  33.4 5.0 %collective-permute-start.10 = (bf16[16,8192]{1,0:T(8,128)(2,1)S(1)}, bf16[16,8192]{1,0:T(8,128)(2,1)S(1)}, u32[]{:S(2)}, u32[]{:S(2)}) collective-permute-start(bf16[16,8192]{1,0:T(8,128)(2,1)S(1)} %collective-permute-done.4.refs_2_), channel_id=1, source_target_pairs={{8,0},{0,8},{24,16},{16,24},{40,32},{32,40},{56,48},{48,56},{72,64... | collective-permute-start | bytes 786440 | tf_op jit(solution)/shard_map/ppermute | solution.py:22
  33.4 4.8 %collective-permute-start.18 = (bf16[16,4096]{1,0:T(8,128)(2,1)S(1)}, bf16[16,4096]{1,0:T(8,128)(2,1)S(1)}, u32[]{:S(2)}, u32[]{:S(2)}) collective-permute-start(bf16[16,4096]{1,0:T(8,128)(2,1)S(1)} %collective-permute-done.14.refs_12_), channel_id=1, source_target_pairs={{8,0},{0,8},{24,16},{16,24},{40,32},{32,40},{56,48},{48,56},{72,64... | collective-permute-start | bytes 393224 | tf_op jit(solution)/shard_map/ppermute | solution.py:22
  33.9 4.9 %collective-permute-start.19 = (bf16[16,4096]{1,0:T(8,128)(2,1)S(1)}, bf16[16,4096]{1,0:T(8,128)(2,1)S(1)}, u32[]{:S(2)}, u32[]{:S(2)}) collective-permute-start(bf16[16,4096]{1,0:T(8,128)(2,1)S(1)} %collective-permute-done.15.refs_13_), channel_id=1, source_target_pairs={{8,0},{0,8},{24,16},{16,24},{40,32},{32,40},{56,48},{48,56},{72,64... | collective-permute-start | bytes 393224 | tf_op jit(solution)/shard_map/ppermute | solution.py:22
  34.0 5.8 %collective-permute-start.16 = (bf16[16,4096]{1,0:T(8,128)(2,1)S(1)}, bf16[16,4096]{1,0:T(8,128)(2,1)S(1)}, u32[]{:S(2)}, u32[]{:S(2)}) collective-permute-start(bf16[16,4096]{1,0:T(8,128)(2,1)S(1)} %slice.42), channel_id=1, source_target_pairs={{16,0},{24,8},{0,16},{8,24},{48,32},{56,40},{32,48},{40,56},{80,64... | collective-permute-start | bytes 393224 | tf_op jit(solution)/shard_map/ppermute | solution.py:22
  34.3 6.8 %collective-permute-start.17 = (bf16[16,4096]{1,0:T(8,128)(2,1)S(1)}, bf16[16,4096]{1,0:T(8,128)(2,1)S(1)}, u32[]{:S(2)}, u32[]{:S(2)}) collective-permute-start(bf16[16,4096]{1,0:T(8,128)(2,1)S(1)} %slice.43), channel_id=1, source_target_pairs={{48,0},{56,8},{32,16},{40,24},{16,32},{24,40},{0,48},{8,56},{112,6... | collective-permute-start | bytes 393224 | tf_op jit(solution)/shard_map/ppermute | solution.py:22
  38.2 24.6 %collective-permute-start.9 = (bf16[16,8192]{1,0:T(8,128)(2,1)S(1)}, bf16[16,8192]{1,0:T(8,128)(2,1)S(1)}, u32[]{:S(2)}, u32[]{:S(2)}) collective-permute-start(bf16[16,8192]{1,0:T(8,128)(2,1)S(1)} %collective-permute-done.3.refs_1_), channel_id=1, source_target_pairs={{8,0},{0,8},{24,16},{16,24},{40,32},{32,40},{56,48},{48,56},{72,64... | collective-permute-start | bytes 786440 | tf_op jit(solution)/shard_map/ppermute | solution.py:22
  38.4 24.4 %collective-permute-start.13 = (bf16[16,8192]{1,0:T(8,128)(2,1)S(1)}, bf16[16,8192]{1,0:T(8,128)(2,1)S(1)}, u32[]{:S(2)}, u32[]{:S(2)}) collective-permute-start(bf16[16,8192]{1,0:T(8,128)(2,1)S(1)} %collective-permute-done.7.refs_5_), channel_id=1, source_target_pairs={{8,0},{0,8},{24,16},{16,24},{40,32},{32,40},{56,48},{48,56},{72,64... | collective-permute-start | bytes 786440 | tf_op jit(solution)/shard_map/ppermute | solution.py:22
  38.8 24.1 %collective-permute-start.12 = (bf16[16,8192]{1,0:T(8,128)(2,1)S(1)}, bf16[16,8192]{1,0:T(8,128)(2,1)S(1)}, u32[]{:S(2)}, u32[]{:S(2)}) collective-permute-start(bf16[16,8192]{1,0:T(8,128)(2,1)S(1)} %collective-permute-done.6.refs_4_), channel_id=1, source_target_pairs={{8,0},{0,8},{24,16},{16,24},{40,32},{32,40},{56,48},{48,56},{72,64... | collective-permute-start | bytes 786440 | tf_op jit(solution)/shard_map/ppermute | solution.py:22
  39.8 23.0 %collective-permute-start.20 = (bf16[16,4096]{1,0:T(8,128)(2,1)S(1)}, bf16[16,4096]{1,0:T(8,128)(2,1)S(1)}, u32[]{:S(2)}, u32[]{:S(2)}) collective-permute-start(bf16[16,4096]{1,0:T(8,128)(2,1)S(1)} %collective-permute-done.16.refs_14_), channel_id=1, source_target_pairs={{8,0},{0,8},{24,16},{16,24},{40,32},{32,40},{56,48},{48,56},{72,64... | collective-permute-start | bytes 393224 | tf_op jit(solution)/shard_map/ppermute | solution.py:22
  41.1 21.8 %collective-permute-start.21 = (bf16[16,4096]{1,0:T(8,128)(2,1)S(1)}, bf16[16,4096]{1,0:T(8,128)(2,1)S(1)}, u32[]{:S(2)}, u32[]{:S(2)}) collective-permute-start(bf16[16,4096]{1,0:T(8,128)(2,1)S(1)} %collective-permute-done.17.refs_15_), channel_id=1, source_target_pairs={{8,0},{0,8},{24,16},{16,24},{40,32},{32,40},{56,48},{48,56},{72,64... | collective-permute-start | bytes 393224 | tf_op jit(solution)/shard_map/ppermute | solution.py:22
  41.1 3.4 %copy-start = (bf16[1,128,32768]{2,1,0:T(8,128)(2,1)S(1)}, bf16[1,128,32768]{2,1,0:T(8,128)(2,1)}, u32[]{:S(2)}) copy-start(bf16[1,128,32768]{2,1,0:T(8,128)(2,1)} %act_ref.1) | copy-start | bytes 25165828
  44.5 2.2 %copy-start.1 = (bf16[1,64,32768]{2,1,0:T(8,128)(2,1)S(1)}, bf16[1,64,32768]{2,1,0:T(8,128)(2,1)}, u32[]{:S(2)}) copy-start(bf16[1,64,32768]{2,1,0:T(8,128)(2,1)} %grad_ref.1) | copy-start | bytes 12582916
  68.9 10.1 %collective-permute-start.22 = (f32[256,256]{1,0:T(8,128)S(1)}, f32[256,256]{1,0:T(8,128)S(1)}, u32[]{:S(2)}, u32[]{:S(2)}) collective-permute-start(f32[256,256]{1,0:T(8,128)S(1)} %slice.45), channel_id=1, source_target_pairs={{6,0},{7,1},{4,2},{5,3},{2,4},{3,5},{0,6},{1,7},{14,8},{15,9},{12,... | collective-permute-start | bytes 786440 | tf_op jit(solution)/shard_map/ppermute | solution.py:22
  79.0 5.3 %collective-permute-start.23 = (f32[128,256]{1,0:T(8,128)S(1)}, f32[128,256]{1,0:T(8,128)S(1)}, u32[]{:S(2)}, u32[]{:S(2)}) collective-permute-start(f32[128,256]{1,0:T(8,128)S(1)} %slice.47), channel_id=1, source_target_pairs={{2,0},{3,1},{0,2},{1,3},{6,4},{7,5},{4,6},{5,7},{10,8},{11,9},{8,1... | collective-permute-start | bytes 393224 | tf_op jit(solution)/shard_map/ppermute | solution.py:22
  85.0 4.3 %collective-permute-start.24 = (f32[64,256]{1,0:T(8,128)S(1)}, f32[64,256]{1,0:T(8,128)S(1)}, u32[]{:S(2)}, u32[]{:S(2)}) collective-permute-start(f32[64,256]{1,0:T(8,128)S(1)} %get-tuple-element.5), channel_id=1, source_target_pairs={{1,0},{0,1},{3,2},{2,3},{5,4},{4,5},{7,6},{6,7},{9,8},{8,9},{11,10... | collective-permute-start | bytes 196616 | tf_op jit(solution)/shard_map/ppermute | solution.py:22
  89.3 0.6 copy-start.5
